TPU v7x, 32 devices: a whole 2x2x4 slice. The times are simulated.
32 devices in a mesh: dp: 8 (over y, x, core), tensor: 4 (over z).
Axes of the slice: x: 2, y: 2, z: 4, core: 2. Of those that a mesh axis runs over, the one named last changes fastest.
Arguments:
- tokens: bfloat16 [4096, 768], P(('dp', 'tensor')), may hold values from -2.5 to 2.5
- condition: bfloat16 [8, 768], P('dp'), may hold values from -2.5 to 2.5
- modulate_weight: bfloat16 [768, 4608], P(None, 'tensor'), may hold values from -0.21875 to 0.21875
- modulate_bias: float32 [4608], P('tensor'), may hold values from -0.75 to 0.75
- heads_weight: bfloat16 [3, 768, 768], P(None, None, 'tensor'), may hold values from -0.21875 to 0.21875
- heads_bias: float32 [2, 768], P(None, 'tensor'), may hold values from -0.75 to 0.75
- output_weight: bfloat16 [768, 768], P('tensor'), may hold values from -0.875 to 0.875
- output_bias: float32 [768], replicated, may hold values from -0.75 to 0.75
- first_weight: bfloat16 [768, 3072], P(None, 'tensor'), may hold values from -0.21875 to 0.21875
- first_bias: float32 [3072], P('tensor'), may hold values from -0.75 to 0.75
- second_weight: bfloat16 [3072, 768], P('tensor'), may hold values from -0.109375 to 0.109375
- second_bias: float32 [768], replicated, may hold values from -0.75 to 0.75
- cotangent: bfloat16 [4096, 768], P(('dp', 'tensor')), may hold values from -2.5 to 2.5
Outputs:
- output: bfloat16 [4096, 768], P(('dp', 'tensor'))
- token_grad: float32 [4096, 768], P(('dp', 'tensor'))
- modulate_weight_grad: float32 [768, 4608], P('dp', 'tensor')
- modulate_bias_grad: float32 [4608], P('tensor')
- heads_weight_grad: float32 [3, 768, 768], P(None, 'dp', 'tensor')
- heads_bias_grad: float32 [2, 768], P(None, 'tensor')
- output_weight_grad: float32 [768, 768], P('tensor', 'dp')
- output_bias_grad: float32 [768], replicated
- first_weight_grad: float32 [768, 3072], P('dp', 'tensor')
- first_bias_grad: float32 [3072], P('tensor')
- second_weight_grad: float32 [3072, 768], P('tensor', 'dp')
- second_bias_grad: float32 [768], replicated
All inputs are finite; a program needn't handle non-finite values.
Results may differ from a plain program's by a relative error of at most 0.012.
The roundings to bfloat16 on the way count: a program that leaves them out, or rounds other values in their place, can miss the bound.
Values may be sent and summed in bfloat16 or wider, within the bound.
A program may use at most 128 MiB of HBM per device.

v0:
```python
from functools import partial
import jax
import jax.numpy as jnp
from jax import lax
from jax.sharding import PartitionSpec as P

HD = 64
LEN = 512
EPSILON = 1e-06
HIGHEST_PRECISION = lax.Precision.HIGHEST


def layer_norm(values):
    centred = values - jnp.mean(values, axis=-1, keepdims=True)
    inverse = lax.rsqrt(jnp.mean(centred * centred, axis=-1, keepdims=True) + EPSILON)
    return (centred * inverse, inverse)


def norm_back(grade, normed, inverse):
    return inverse * (
        grade
        - jnp.mean(grade, axis=-1, keepdims=True)
        - normed * jnp.mean(grade * normed, axis=-1, keepdims=True)
    )


def matmul(left, right):
    return jnp.dot(left, right, preferred_element_type=jnp.float32)


def left_contract(left, right):
    return lax.dot_general(
        left, right, (((0,), (0,)), ((), ())), preferred_element_type=jnp.float32
    )


def right_contract(left, right):
    return lax.dot_general(
        left, right, (((1,), (1,)), ((), ())), preferred_element_type=jnp.float32
    )


def exact_left(left, right):
    return lax.dot_general(
        left,
        right,
        (((0,), (0,)), ((), ())),
        precision=HIGHEST_PRECISION,
        preferred_element_type=jnp.float32,
    )


def head_cols(values, head):
    return values[:, head * HD : (head + 1) * HD]


def attend_forward(blocks):
    query_block, key_block, value_block = blocks
    outputs = []
    sums = []
    for head in range(query_block.shape[1] // HD):
        scores = right_contract(head_cols(query_block, head), head_cols(key_block, head)) * HD ** (
            -0.5
        )
        peak = jnp.max(scores, axis=-1, keepdims=True)
        expo = jnp.exp(scores - peak)
        total = jnp.sum(expo, axis=-1, keepdims=True)
        probability = (expo / total).astype(jnp.bfloat16)
        outputs.append(matmul(probability, head_cols(value_block, head)))
        sums.append((peak + jnp.log(total))[:, 0])
    return (jnp.concatenate(outputs, axis=1).astype(jnp.bfloat16), jnp.stack(sums))


def attend_backward(blocks):
    query_block, key_block, value_block, grade_block, logsum = blocks
    query_parts = []
    key_parts = []
    value_parts = []
    for head in range(query_block.shape[1] // HD):
        query_head = head_cols(query_block, head)
        key_head = head_cols(key_block, head)
        grade_head = head_cols(grade_block, head)
        scores = right_contract(query_head, key_head) * HD ** (-0.5)
        probability = jnp.exp(scores - logsum[head][:, None])
        value_parts.append(left_contract(probability.astype(jnp.bfloat16), grade_head))
        prob_grad = right_contract(grade_head, head_cols(value_block, head))
        score_grad = probability * (
            prob_grad - jnp.sum(probability * prob_grad, axis=-1, keepdims=True)
        )
        score_low = score_grad.astype(jnp.bfloat16)
        query_parts.append(matmul(score_low, key_head) * HD ** (-0.5))
        key_parts.append(left_contract(score_low, query_head) * HD ** (-0.5))
    return jnp.stack(
        [
            jnp.concatenate(query_parts, axis=1),
            jnp.concatenate(key_parts, axis=1),
            jnp.concatenate(value_parts, axis=1),
        ]
    ).astype(jnp.bfloat16)


def local(
    tokens,
    condition,
    modulate_weight,
    modulate_bias,
    heads_weight,
    heads_bias,
    output_weight,
    output_bias,
    first_weight,
    first_bias,
    second_weight,
    second_bias,
    cotangent,
):
    tensor_rank = lax.axis_index("tensor")
    row_count = tokens.shape[0]
    model_width = tokens.shape[1]
    latent_count = condition.shape[0]
    local_width = heads_weight.shape[2]
    group_rows = latent_count * LEN
    silu_cond = jax.nn.silu(condition.astype(jnp.float32)).astype(jnp.bfloat16)
    modulate_local = matmul(silu_cond, modulate_weight) + modulate_bias
    modulation = lax.all_gather(modulate_local, "tensor", axis=1, tiled=True)
    latent_of_row = (tensor_rank * row_count + jnp.arange(row_count, dtype=jnp.int32)) // LEN
    selector = (
        latent_of_row[:, None] == jnp.arange(latent_count, dtype=jnp.int32)[None, :]
    ).astype(jnp.float32)
    row_mods = jnp.dot(selector, modulation, precision=HIGHEST_PRECISION)
    pieces = [row_mods[:, member * model_width : (member + 1) * model_width] for member in range(6)]
    shift_attn, scale_attn, gate_attn, shift_feed, scale_feed, gate_feed = pieces
    residual = tokens.astype(jnp.float32)
    normed_first, inverse_first = layer_norm(residual)
    attention_in = (normed_first * (1.0 + scale_attn) + shift_attn).astype(jnp.bfloat16)
    attention_all = lax.all_gather(attention_in, "tensor", axis=0, tiled=True)
    projected = jnp.einsum(
        "td,sde->ste", attention_all, heads_weight, preferred_element_type=jnp.float32
    )
    query_rows = (projected[0] + heads_bias[0]).astype(jnp.bfloat16)
    key_rows = projected[1].astype(jnp.bfloat16)
    value_rows = (projected[2] + heads_bias[1]).astype(jnp.bfloat16)
    shaped = (latent_count, LEN, local_width)
    query_blocks = query_rows.reshape(shaped)
    key_blocks = key_rows.reshape(shaped)
    value_blocks = value_rows.reshape(shaped)
    mixture, logsum = lax.map(attend_forward, (query_blocks, key_blocks, value_blocks))
    mixture = mixture.reshape(group_rows, local_width)
    branch_attn = (
        lax.psum_scatter(
            matmul(
                lax.slice_in_dim(mixture, 0, lax.axis_size("tensor") * row_count, axis=0),
                output_weight,
            ),
            "tensor",
            scatter_dimension=0,
            tiled=True,
        )
        + output_bias
    )
    residual_mid = residual + gate_attn * branch_attn
    normed_second, inverse_second = layer_norm(residual_mid)
    feed_in = (normed_second * (1.0 + scale_feed) + shift_feed).astype(jnp.bfloat16)
    feed_all = lax.all_gather(feed_in, "tensor", axis=0, tiled=True)
    hidden_pre = matmul(feed_all, first_weight) + first_bias
    activated = jax.nn.gelu(hidden_pre, approximate=True).astype(jnp.bfloat16)
    branch_feed = (
        lax.psum_scatter(
            matmul(
                lax.slice_in_dim(activated, 0, lax.axis_size("tensor") * row_count, axis=0),
                second_weight,
            ).astype(jnp.bfloat16),
            "tensor",
            scatter_dimension=0,
            tiled=True,
        ).astype(jnp.float32)
        + second_bias
    )
    output = (residual_mid + gate_feed * branch_feed).astype(jnp.bfloat16)
    tangent = cotangent.astype(jnp.float32)
    feed_grad = (gate_feed * tangent).astype(jnp.bfloat16)
    feed_grad_all = lax.all_gather(feed_grad, "tensor", axis=0, tiled=True)
    grad_second_bias = jnp.sum(feed_grad_all, axis=0, dtype=jnp.float32)
    grad_second_weight = left_contract(activated, feed_grad_all)
    activated_grad = right_contract(feed_grad_all, second_weight)
    unused_value, gelu_back = jax.vjp(partial(jax.nn.gelu, approximate=True), hidden_pre)
    pre_grad = gelu_back(activated_grad)[0].astype(jnp.bfloat16)
    grad_first_bias = jnp.sum(pre_grad, axis=0, dtype=jnp.float32)
    grad_first_weight = left_contract(feed_all, pre_grad)
    feed_in_grad = lax.psum_scatter(
        right_contract(
            lax.slice_in_dim(pre_grad, 0, lax.axis_size("tensor") * row_count, axis=0), first_weight
        ),
        "tensor",
        scatter_dimension=0,
        tiled=True,
    )
    mid_grad = tangent + norm_back(feed_in_grad * (1.0 + scale_feed), normed_second, inverse_second)
    attn_grad = (gate_attn * mid_grad).astype(jnp.bfloat16)
    attn_grad_all = lax.all_gather(attn_grad, "tensor", axis=0, tiled=True)
    grad_output_bias = jnp.sum(attn_grad_all, axis=0, dtype=jnp.float32)
    grad_output_weight = left_contract(mixture, attn_grad_all)
    mixture_grad = right_contract(attn_grad_all, output_weight).astype(jnp.bfloat16)
    stacked_grads = lax.map(
        attend_backward,
        (query_blocks, key_blocks, value_blocks, mixture_grad.reshape(shaped), logsum),
    )
    heads_grad = jnp.swapaxes(stacked_grads, 0, 1).reshape(3, group_rows, local_width)
    grad_heads_weight = jnp.einsum(
        "td,ste->sde", attention_all, heads_grad, preferred_element_type=jnp.float32
    )
    grad_heads_bias = jnp.stack(
        [
            jnp.sum(heads_grad[0], axis=0, dtype=jnp.float32),
            jnp.sum(heads_grad[2], axis=0, dtype=jnp.float32),
        ]
    )
    attn_in_grad = lax.psum_scatter(
        jnp.einsum("ste,sde->td", heads_grad, heads_weight, preferred_element_type=jnp.float32),
        "tensor",
        scatter_dimension=0,
        tiled=True,
    )
    token_grad = mid_grad + norm_back(
        attn_in_grad * (1.0 + scale_attn), normed_first, inverse_first
    )
    row_terms = jnp.concatenate(
        [
            attn_in_grad,
            attn_in_grad * normed_first,
            mid_grad * branch_attn,
            feed_in_grad,
            feed_in_grad * normed_second,
            tangent * branch_feed,
        ],
        axis=1,
    )
    modulation_partial = exact_left(selector, row_terms)
    modulation_grad = lax.psum_scatter(
        modulation_partial, "tensor", scatter_dimension=1, tiled=True
    )
    grad_modulate_bias = jnp.sum(modulation_grad, axis=0)
    bias_total = lax.psum(
        (grad_modulate_bias, grad_heads_bias, grad_output_bias, grad_first_bias, grad_second_bias),
        "dp",
    )
    cond_all, modulation_all = (
        lax.all_gather(silu_cond.astype(jnp.float32), "dp", axis=0, tiled=True),
        lax.all_gather(modulation_grad, "dp", axis=0, tiled=True),
    )
    share = model_width // lax.axis_size("dp")
    cond_share = lax.dynamic_slice_in_dim(cond_all, lax.axis_index("dp") * share, share, 1)
    grad_modulate_weight = exact_left(cond_share, modulation_all)
    matrices = (
        lax.psum_scatter(grad_heads_weight, "dp", scatter_dimension=1, tiled=True),
        lax.psum_scatter(grad_output_weight, "dp", scatter_dimension=1, tiled=True),
        lax.psum_scatter(grad_first_weight, "dp", scatter_dimension=0, tiled=True),
        lax.psum_scatter(grad_second_weight, "dp", scatter_dimension=1, tiled=True),
    )
    return (
        output,
        token_grad,
        grad_modulate_weight,
        bias_total[0],
        matrices[0],
        bias_total[1],
        matrices[1],
        bias_total[2],
        matrices[2],
        bias_total[3],
        matrices[3],
        bias_total[4],
    )


def solution(mesh):
    in_specs = (
        P(("dp", "tensor"), None),
        P("dp", None),
        P(None, "tensor"),
        P("tensor"),
        P(None, None, "tensor"),
        P(None, "tensor"),
        P("tensor", None),
        P(),
        P(None, "tensor"),
        P("tensor"),
        P("tensor", None),
        P(),
        P(("dp", "tensor"), None),
    )
    out_specs = (
        P(("dp", "tensor"), None),
        P(("dp", "tensor"), None),
        P("dp", "tensor"),
        P("tensor"),
        P(None, "dp", "tensor"),
        P(None, "tensor"),
        P("tensor", "dp"),
        P(),
        P("dp", "tensor"),
        P("tensor"),
        P("tensor", "dp"),
        P(),
    )
    return jax.shard_map(local, mesh=mesh, in_specs=in_specs, out_specs=out_specs, check_vma=False)
```

profile of v0, /device:TPU:0, one launch (start us, length us, event | category | flops | bytes accessed | tf_op | source)
XLA Modules:
  0.0 488.1 jit_solution(5927712620343426322)
XLA Ops:
  7.3 1.2 convert_reduce_fusion.3
  8.4 1.1 fusion.39
  9.6 0.8 fusion.100
  10.4 1.0 convolution_reduce_fusion
  11.4 14.9 %all-gather.1 = f32[4,1,1152]{2,1,0:T(1,128)S(1)} all-gather(f32[1,1,1152]{2,1,0:T(1,128)S(1)} %reshape.153), channel_id=2, replica_groups=mesh['dp'=8,'tensor'=4] {'tensor'}, dimensions={0}, use_global_device_ids=true | all-gather | bytes 23040 | tf_op jit(solution)/shard_map/all_gather | solution.py:125
  27.0 17.7 %all_gather.22 = bf16[512,768]{1,0:T(8,128)(2,1)S(1)} all-gather(bf16[128,768]{1,0:T(8,128)(2,1)S(1)} %fusion.33), channel_id=1, replica_groups=mesh['dp'=8,'tensor'=4] {'tensor'}, dimensions={0}, use_global_device_ids=true | all-gather | bytes 983040 | tf_op jit(solution)/shard_map/all_gather | solution.py:136
  44.7 0.7 fusion.104
  46.5 0.4 fusion.103
  49.2 0.4 copy-done.21
  49.6 1.6 fusion.50
  51.3 35.5 %reduce-scatter.16.cloned.1.call-done = f32[128,768]{1,0:T(8,128)} async-done(((f32[512,768]{1,0:T(8,128)}), f32[128,768]{1,0:T(8,128)}) %reduce-scatter.16.cloned.1.call-update) | async-done | bytes 393232 | tf_op jit(solution)/shard_map/reduce_scatter | solution.py:150
  86.8 1.3 fusion.99
  88.3 1.6 fusion.40
  89.9 18.1 %all_gather.24 = bf16[512,768]{1,0:T(8,128)(2,1)S(1)} all-gather(bf16[128,768]{1,0:T(8,128)(2,1)S(1)} %get-tuple-element.91), channel_id=1, replica_groups=mesh['dp'=8,'tensor'=4] {'tensor'}, dimensions={0}, use_global_device_ids=true | all-gather | bytes 983040 | tf_op jit(solution)/shard_map/all_gather | solution.py:182
  108.0 17.5 %all_gather.23 = bf16[512,768]{1,0:T(8,128)(2,1)S(1)} all-gather(bf16[128,768]{1,0:T(8,128)(2,1)S(1)} %get-tuple-element.92), channel_id=1, replica_groups=mesh['dp'=8,'tensor'=4] {'tensor'}, dimensions={0}, use_global_device_ids=true | all-gather | bytes 983040 | tf_op jit(solution)/shard_map/all_gather | solution.py:164
  125.6 0.8 fusion.105
  126.4 0.7 copy-done.64
  127.1 3.4 convert_reduce_fusion.1
  130.5 0.9 copy-done.27
  131.4 2.0 fusion.106
  133.5 3.8 convolution_convert_fusion
  137.3 0.7 log_add_fusion.1
  138.0 0.7 log_add_fusion.2
  138.7 29.7 %reduce-scatter.20.cloned.1.call-done = f32[128,768]{1,0:T(8,128)} async-done(((f32[512,768]{1,0:T(8,128)}), f32[128,768]{1,0:T(8,128)}) %reduce-scatter.20.cloned.1.call-update) | async-done | bytes 393232 | tf_op jit(solution)/shard_map/reduce_scatter | solution.py:190
  168.5 1.3 fusion.95
  169.8 0.5 broadcast_multiply_fusion.3
  170.3 22.8 %reduce-scatter.18.cloned.1.call-done = bf16[128,768]{1,0:T(8,128)(2,1)} async-done(((bf16[512,768]{1,0:T(8,128)(2,1)}), bf16[128,768]{1,0:T(8,128)(2,1)}) %reduce-scatter.18.cloned.1.call-update) | async-done | bytes 196624 | tf_op jit(solution)/shard_map/reduce_scatter | solution.py:168
  193.1 2.5 multiply_convert_fusion.4
  195.7 18.3 %all_gather.25 = bf16[512,768]{1,0:T(8,128)(2,1)S(1)} all-gather(bf16[128,768]{1,0:T(8,128)(2,1)S(1)} %get-tuple-element.86), channel_id=1, replica_groups=mesh['dp'=8,'tensor'=4] {'tensor'}, dimensions={0}, use_global_device_ids=true | all-gather | bytes 983040 | tf_op jit(solution)/shard_map/all_gather | solution.py:200
  213.9 0.4 convolution_convert_fusion.1
  214.7 0.4 multiply_reduce_fusion
  215.4 0.6 copy-done.15
  216.8 0.4 multiply_reduce_fusion.1
  219.8 0.4 copy-done.43
  220.2 0.7 copy-done.44
  220.9 2.0 convolution_bitcast_fusion.2
  223.0 1.1 copy-done.7
  224.1 1.4 convolution_bitcast_fusion.3
  225.6 3.2 convolution_bitcast_fusion.1
  228.8 4.2 copy.29
  233.0 4.7 reshape.172
  237.8 19.9 %reduce-scatter.22.cloned.1.call-done = f32[128,768]{1,0:T(8,128)} async-done(((f32[512,768]{1,0:T(8,128)}), f32[128,768]{1,0:T(8,128)}) %reduce-scatter.22.cloned.1.call-update) | async-done | bytes 393232 | tf_op jit(solution)/shard_map/reduce_scatter | solution.py:218
  257.7 1.4 fusion.96
  259.1 2.0 fusion.38
  261.4 0.7 copy-done.18
  262.2 3.5 convolution_bitcast_fusion
  265.8 4.2 fusion.97
  270.1 3.6 fusion.107
  273.7 0.6 copy-done.51
  274.3 9.2 %all-gather.2 = f32[8,1,768]{2,1,0:T(1,128)S(1)} all-gather(f32[1,1,768]{2,1,0:T(1,128)S(1)} %bitcast_convert_fusion), channel_id=1, replica_groups=mesh['dp'=8,'tensor'=4] {'dp'}, dimensions={0}, use_global_device_ids=true | all-gather | bytes 27648 | tf_op jit(solution)/shard_map/all_gather | solution.py:248
  283.6 1.3 convert_reduce_fusion
  285.4 9.2 %reduce-scatter.32.cloned.1.call-done = f32[96,192]{1,0:T(8,128)} async-done(((f32[768,192]{1,0:T(8,128)}), f32[96,192]{1,0:T(8,128)}) %reduce-scatter.32.cloned.1.call-update) | async-done | bytes 73744
  294.6 1.6 copy.32
  296.3 42.0 %reduce-scatter.30.cloned.1.call-done = f32[96,576]{1,0:T(8,128)} async-done(((f32[768,576]{1,0:T(8,128)}), f32[96,576]{1,0:T(8,128)}) %reduce-scatter.30.cloned.1.call-update) | async-done | bytes 221200
  338.2 1.1 reshape.173
  339.4 0.8 copy.26
  340.1 48.6 %reduce-scatter.28.cloned.1.call-done = f32[1152,1]{1,0:T(8,128)} async-done(((f32[4608,1]{1,0:T(8,128)}), f32[1152,1]{1,0:T(8,128)}) %reduce-scatter.28.cloned.1.call-update) | async-done | bytes 4624
  388.7 1.3 copy.28
  389.9 1.3 bitcast_reduce_fusion
  391.3 24.4 %all-reduce = (f32[1152]{0:T(1024)}, f32[2,192]{1,0:T(2,128)}, f32[768]{0:T(1024)}, f32[768]{0:T(1024)}, f32[768]{0:T(1024)}) all-reduce(f32[1152]{0:T(1024)S(1)} %bitcast_reduce_fusion, f32[2,192]{1,0:T(2,128)S(1)} %pad_maximum_fusion.6, f32[768]{0:T(1024)S(1)} %convert_reduce_fusion.2, ...), channel_id=1, replica_groups=mesh['dp'=8,'tensor'=4] {'dp'}, use_global_device_ids=true, to_apply=%region_22.23 | all-reduce | flops 3840 | bytes 30720 | tf_op jit(solution)/shard_map/psum | solution.py:243
  415.7 8.1 %all-gather.3 = f32[8,1,1152]{2,1,0:T(1,128)S(1)} all-gather(f32[1,1,1152]{2,1,0:T(1,128)S(1)} %bitcast.98), channel_id=1, replica_groups=mesh['dp'=8,'tensor'=4] {'dp'}, dimensions={0}, use_global_device_ids=true | all-gather | bytes 41472 | tf_op jit(solution)/shard_map/all_gather | solution.py:249
  423.8 1.3 fusion.78
  425.2 10.0 %reduce-scatter.26.cloned.1.call-done = f32[768,96]{0,1:T(8,128)} async-done(((f32[768,768]{0,1:T(8,128)}), f32[768,96]{0,1:T(8,128)}) %reduce-scatter.26.cloned.1.call-update) | async-done | bytes 294928 | tf_op jit(solution)/shard_map/reduce_scatter | solution.py:258
  435.1 46.5 %reduce-scatter.24.cloned.1.call-done = f32[96,768]{1,0:T(8,128)} async-done(((f32[768,768]{1,0:T(8,128)}), f32[96,768]{1,0:T(8,128)}) %reduce-scatter.24.cloned.1.call-update) | async-done | bytes 294928 | tf_op jit(solution)/shard_map/reduce_scatter | solution.py:257
  (194 shorter events, 9.5 us)
Async XLA Ops:
  7.2 3.2 copy-start
  7.2 4.2 copy-start.58
  7.2 79.6 %reduce-scatter.16.cloned.1.call-start = ((), (), s32[]{:S(2)}) async-start(), calls=%async_computation.9 | async-start | bytes 1966080 | tf_op jit(solution)/shard_map/reduce_scatter | solution.py:150
  8.4 18.3 %copy-start.52 = (f32[128]{0:T(128)}, f32[128]{0:T(128)S(1)}, u32[]{:S(2)}) copy-start(f32[128]{0:T(128)S(1)} %broadcast_multiply_fusion.6) | copy-start | bytes 1540
  9.6 17.2 %copy-start.61 = (f32[128]{0:T(128)}, f32[128]{0:T(128)S(1)}, u32[]{:S(2)}) copy-start(f32[128]{0:T(128)S(1)} %add_rsqrt_fusion.1) | copy-start | bytes 1540
  11.4 15.4 %copy-start.8 = (bf16[128,768]{1,0:T(8,128)(2,1)S(1)}, bf16[128,768]{1,0:T(8,128)(2,1)}, u32[]{:S(2)}) copy-start(bf16[128,768]{1,0:T(8,128)(2,1)} %param.13) | copy-start | bytes 589828
  26.8 18.6 %copy-start.5 = (f32[128,4608]{1,0:T(8,128)}, f32[128,4608]{1,0:T(8,128)S(1)}, u32[]{:S(2)}) copy-start(f32[128,4608]{1,0:T(8,128)S(1)} %broadcast_multiply_fusion) | copy-start | bytes 7077892
  26.8 18.0 %copy-start.23 = (bf16[3,768,192]{1,2,0:T(8,128)(2,1)S(1)}, bf16[3,768,192]{1,2,0:T(8,128)(2,1)}, u32[]{:S(2)}) copy-start(bf16[3,768,192]{1,2,0:T(8,128)(2,1)} %param.17) | copy-start | bytes 2654212
  45.7 1.1 copy-start.16
  45.7 2.9 copy-start.25
  46.1 1.0 copy-start.3
  46.5 1.4 copy-start.1
  46.9 1.8 copy-start.45
  48.6 1.0 copy-start.21
  49.6 1.6 copy-start.41
  49.6 37.1 %copy-start.46 = (f32[768]{0:T(1024)S(1)}, f32[768]{0:T(1024)}, u32[]{:S(2)}) copy-start(f32[768]{0:T(1024)} %param.20) | copy-start | bytes 9220
  51.2 117.2 %reduce-scatter.20.cloned.1.call-start = ((), (), s32[]{:S(2)}) async-start(), calls=%async_computation.11 | async-start | bytes 1966080 | tf_op jit(solution)/shard_map/reduce_scatter | solution.py:190
  88.0 20.0 %copy-start.49 = (f32[128]{0:T(128)}, f32[128]{0:T(128)S(1)}, u32[]{:S(2)}) copy-start(f32[128]{0:T(128)S(1)} %broadcast_multiply_fusion.5) | copy-start | bytes 1540
  88.2 19.8 %copy-start.59 = (f32[128]{0:T(128)}, f32[128]{0:T(128)S(1)}, u32[]{:S(2)}) copy-start(f32[128]{0:T(128)S(1)} %add_rsqrt_fusion) | copy-start | bytes 1540
  88.3 37.3 %copy-start.65 = (bf16[768,768]{1,0:T(8,128)(2,1)S(1)}, bf16[768,768]{1,0:T(8,128)(2,1)}, u32[]{:S(2)}) copy-start(bf16[768,768]{1,0:T(8,128)(2,1)} %param.23) | copy-start | bytes 3538948
  108.0 17.5 %copy-start.12 = (bf16[512,768]{1,0:T(8,128)(2,1)}, bf16[512,768]{1,0:T(8,128)(2,1)S(1)}, u32[]{:S(2)}) copy-start(bf16[512,768]{1,0:T(8,128)(2,1)S(1)} %all_gather.24) | copy-start | bytes 2359300
  125.5 1.6 copy-start.64
  125.6 1.5 copy-start.66
  133.4 59.7 %reduce-scatter.18.cloned.1.call-start = ((), (), s32[]{:S(2)}) async-start(), calls=%async_computation.10 | async-start | bytes 983040 | tf_op jit(solution)/shard_map/reduce_scatter | solution.py:168
  133.5 3.9 copy-start.55
  137.3 120.4 %reduce-scatter.22.cloned.1.call-start = ((), (), s32[]{:S(2)}) async-start(), calls=%async_computation.12 | async-start | bytes 1966080 | tf_op jit(solution)/shard_map/reduce_scatter | solution.py:218
  193.1 20.8 %copy-start.22 = (bf16[192,768]{1,0:T(8,128)(2,1)S(1)}, bf16[192,768]{1,0:T(8,128)(2,1)}, u32[]{:S(2)}) copy-start(bf16[192,768]{1,0:T(8,128)(2,1)} %param.19) | copy-start | bytes 884740
  195.7 18.7 %copy-start.4 = (f32[512,512]{0,1:T(8,128)S(1)}, f32[512,512]{0,1:T(8,128)}, u32[]{:S(2)}) copy-start(f32[512,512]{0,1:T(8,128)} %copy-done.3) | copy-start | bytes 3145732
  195.7 19.0 %copy-start.26 = (bf16[512,192]{0,1:T(8,128)(2,1)S(1)}, bf16[512,192]{0,1:T(8,128)(2,1)}, u32[]{:S(2)}) copy-start(bf16[512,192]{0,1:T(8,128)(2,1)} %copy-done.25) | copy-start | bytes 589828
  213.9 1.1 copy-start.6
  214.7 4.8 copy-start.29
  215.1 0.9 copy-start.15
  215.1 1.1 copy-start.17
  215.1 1.4 copy-start.2
  216.2 3.3 copy-start.31
  216.8 2.6 copy-start.33
  217.7 1.8 copy-start.35
  218.3 1.2 copy-start.37
  218.9 2.0 copy-start.24
  222.9 1.1 copy-start.7
  222.9 1.1 copy-start.42
  223.0 71.7 %reduce-scatter.32.cloned.1.call-start = ((), (), s32[]{:S(2)}) async-start(), calls=%async_computation.17 | async-start | bytes 884736
  225.5 112.7 %reduce-scatter.30.cloned.1.call-start = ((), (), s32[]{:S(2)}) async-start(), calls=%async_computation.16 | async-start | bytes 2211840
  237.7 20.0 %copy-start.53 = (f32[128]{0:T(128)S(1)}, f32[128]{0:T(128)}, u32[]{:S(2)}) copy-start(f32[128]{0:T(128)} %copy-done.52) | copy-start | bytes 1540
  237.7 20.0 %copy-start.62 = (f32[128]{0:T(128)S(1)}, f32[128]{0:T(128)}, u32[]{:S(2)}) copy-start(f32[128]{0:T(128)} %copy-done.61) | copy-start | bytes 1540
  237.7 21.4 %copy-start.11 = (f32[128,768]{1,0:T(8,128)S(1)}, f32[128,768]{1,0:T(8,128)}, u32[]{:S(2)}) copy-start(f32[128,768]{1,0:T(8,128)} %get-tuple-element.87) | copy-start | bytes 1179652
  237.7 23.4 %copy-start.47 = (f32[768]{0:T(1024)S(1)}, f32[768]{0:T(1024)}, u32[]{:S(2)}) copy-start(f32[768]{0:T(1024)} %param.20) | copy-start | bytes 9220
  237.7 151.0 %reduce-scatter.28.cloned.1.call-start = ((), (), s32[]{:S(2)}) async-start(), calls=%async_computation.15 | async-start | bytes 2949120
  257.6 1.4 copy-start.19
  257.7 3.5 copy-start.20
  259.1 2.1 copy-start.9
  259.1 2.2 copy-start.50
  259.1 2.2 copy-start.60
  261.1 1.0 copy-start.28
  261.1 1.0 copy-start.48
  265.7 169.4 %reduce-scatter.26.cloned.1.call-start = ((), (), s32[]{:S(2)}) async-start(), calls=%async_computation.14 | async-start | bytes 2654208 | tf_op jit(solution)/shard_map/reduce_scatter | solution.py:258
  270.0 211.6 %reduce-scatter.24.cloned.1.call-start = ((), (), s32[]{:S(2)}) async-start(), calls=%async_computation.13 | async-start | bytes 2654208 | tf_op jit(solution)/shard_map/reduce_scatter | solution.py:257
  273.6 11.3 %copy-start.30 = (bf16[512,64]{0,1:T(8,128)(2,1)S(1)}, bf16[512,64]{0,1:T(8,128)(2,1)}, u32[]{:S(2)}) copy-start(bf16[512,64]{0,1:T(8,128)(2,1)} %copy-done.29) | copy-start | bytes 196612
  273.6 11.3 %copy-start.34 = (bf16[512,64]{0,1:T(8,128)(2,1)S(1)}, bf16[512,64]{0,1:T(8,128)(2,1)}, u32[]{:S(2)}) copy-start(bf16[512,64]{0,1:T(8,128)(2,1)} %copy-done.33) | copy-start | bytes 196612
  273.6 11.3 %copy-start.38 = (bf16[512,64]{0,1:T(8,128)(2,1)S(1)}, bf16[512,64]{0,1:T(8,128)(2,1)}, u32[]{:S(2)}) copy-start(bf16[512,64]{0,1:T(8,128)(2,1)} %copy-done.37) | copy-start | bytes 196612
  273.7 11.4 %copy-start.32 = (bf16[512,64]{0,1:T(8,128)(2,1)S(1)}, bf16[512,64]{0,1:T(8,128)(2,1)}, u32[]{:S(2)}) copy-start(bf16[512,64]{0,1:T(8,128)(2,1)} %copy-done.31) | copy-start | bytes 196612
  273.7 11.4 %copy-start.36 = (bf16[512,64]{0,1:T(8,128)(2,1)S(1)}, bf16[512,64]{0,1:T(8,128)(2,1)}, u32[]{:S(2)}) copy-start(bf16[512,64]{0,1:T(8,128)(2,1)} %copy-done.35) | copy-start | bytes 196612
  273.7 11.4 %copy-start.40 = (bf16[512,64]{0,1:T(8,128)(2,1)S(1)}, bf16[512,64]{0,1:T(8,128)(2,1)}, u32[]{:S(2)}) copy-start(bf16[512,64]{0,1:T(8,128)(2,1)} %copy-done.39) | copy-start | bytes 196612
  285.2 106.0 %copy-start.63 = (f32[768]{0:T(1024)S(1)}, f32[768]{0:T(1024)}, u32[]{:S(2)}) copy-start(f32[768]{0:T(1024)} %get-tuple-element.84) | copy-start | bytes 9220
  (12 other events, 8.9 us)
Sparse Core Ops, SparseCore 0:
  51.3 35.3 reduce-scatter.15
  133.5 34.8 reduce-scatter.19
  170.8 22.3 reduce-scatter.17
  223.1 34.5 reduce-scatter.21
  260.6 33.9 reduce-scatter.31
  297.9 40.2 reduce-scatter.29
  340.6 47.9 reduce-scatter.27
  393.0 42.1 reduce-scatter.25
  439.1 42.4 reduce-scatter.23
where the time goes:
time: 489 us; the launch traced here: 488 us
  waiting for transfers between devices  264 us (54%)
  blocking collectives  128 us (26%)
  matrix products  38.3 us (8%)
  local copies, waits for them, and re-layouts  23.5 us (5%)
  other arithmetic  18.5 us (4%)
  between operations  14.8 us (3%)
    unnamed x12, waiting for transfers between devices  99.9 us
    reduce_scatter x1, waiting for transfers between devices, local(): lax.psum_scatter(grad_first_weight, 'dp', scatter_dimension=0, tiled=True)  46.5 us
    reduce_scatter x1, waiting for transfers between devices, local(): lax.psum_scatter(matmul(lax.slice_in_dim(mixture, 0, lax.axis_size('tenso...  35.5 us
    reduce_scatter x1, waiting for transfers between devices, local(): lax.psum_scatter(right_contract(lax.slice_in_dim(pre_grad, 0, lax.axis_si...  29.7 us
    psum x1, blocking collectives, local(): lax.psum((grad_modulate_bias, grad_heads_bias, grad_output_bias, grad_fir...  24.4 us
    reduce_scatter x1, waiting for transfers between devices, local(): lax.psum_scatter(matmul(lax.slice_in_dim(activated, 0, lax.axis_size('ten...  22.8 us
    unnamed x143, local copies, waits for them, and re-layouts  21.3 us
    reduce_scatter x1, waiting for transfers between devices, local(): lax.psum_scatter(jnp.einsum('ste,sde->td', heads_grad, heads_weight, pref...  19.9 us
  transfers between devices with their start and end apart: 9, of which 9 were waited for; matrix products, arithmetic and copies ran while one was open for 9% of the time, Pallas kernels for 0%

commit v1 on v0

--- a/solution.py
+++ b/solution.py
@@ -161,7 +161,9 @@
     residual_mid = residual + gate_attn * branch_attn
     normed_second, inverse_second = layer_norm(residual_mid)
     feed_in = (normed_second * (1.0 + scale_feed) + shift_feed).astype(jnp.bfloat16)
-    feed_all = lax.all_gather(feed_in, "tensor", axis=0, tiled=True)
+    feed_all = jnp.concatenate(
+        lax.all_to_all(jnp.stack([feed_in] * lax.axis_size("tensor")), "tensor", 0, 0), axis=0
+    )
     hidden_pre = matmul(feed_all, first_weight) + first_bias
     activated = jax.nn.gelu(hidden_pre, approximate=True).astype(jnp.bfloat16)
     branch_feed = (

time: 489 us -> 499 us (1.020)
    all_gather x1 -> x0, blocking collectives: 17.5 us -> none  [local(): feed_all = lax.all_gather(feed_in, 'tensor', axis=0, tiled=True)]
    all_gather x1, blocking collectives: 18.1 us -> 33.7 us  [local(): feed_grad_all = lax.all_gather(feed_grad, 'tensor', axis=0, tiled=True)]
    unnamed x143 -> x139, local copies, waits for them, and re-layouts: 21.3 us -> 21.7 us
  transfers between devices with their start and end apart: 9 -> 10, of which waited for: 9 -> 9; matrix products, arithmetic and copies ran while one was open for 9% -> 10% of each run, Pallas kernels for 0% -> 0%
where the time goes in v1:
time: 499 us; the launch traced here: 498 us
  waiting for transfers between devices  265 us (53%)
  blocking collectives  126 us (25%)
  matrix products  42.9 us (9%)
  local copies, waits for them, and re-layouts  24.8 us (5%)
  other arithmetic  19.1 us (4%)
  between operations  14.7 us (3%)
    unnamed x12, waiting for transfers between devices  99.9 us
    reduce_scatter x1, waiting for transfers between devices, local(): lax.psum_scatter(grad_first_weight, 'dp', scatter_dimension=0, tiled=True)  46.5 us
    reduce_scatter x1, waiting for transfers between devices, local(): lax.psum_scatter(matmul(lax.slice_in_dim(mixture, 0, lax.axis_size('tenso...  35.6 us
    all_gather x1, blocking collectives, local(): feed_grad_all = lax.all_gather(feed_grad, 'tensor', axis=0, tiled=True)  33.7 us
    reduce_scatter x1, waiting for transfers between devices, local(): lax.psum_scatter(right_contract(lax.slice_in_dim(pre_grad, 0, lax.axis_si...  30.5 us
    psum x1, blocking collectives, local(): lax.psum((grad_modulate_bias, grad_heads_bias, grad_output_bias, grad_fir...  24.4 us
    reduce_scatter x1, waiting for transfers between devices, local(): lax.psum_scatter(matmul(lax.slice_in_dim(activated, 0, lax.axis_size('ten...  22.8 us
    unnamed x139, local copies, waits for them, and re-layouts  21.7 us
  transfers between devices with their start and end apart: 10, of which 9 were waited for; matrix products, arithmetic and copies ran while one was open for 10% of the time, Pallas kernels for 0%

profile of v1, /device:TPU:0, one launch (start us, length us, event | category | flops | bytes accessed | tf_op | source)
XLA Modules:
  0.0 497.7 jit_solution(11279027960275689916)
XLA Ops:
  7.3 1.2 convert_reduce_fusion.3
  8.4 1.1 fusion.39
  9.6 0.8 fusion.100
  10.4 1.0 convolution_reduce_fusion
  11.4 14.9 %all-gather.1 = f32[4,1,1152]{2,1,0:T(1,128)S(1)} all-gather(f32[1,1,1152]{2,1,0:T(1,128)S(1)} %reshape.159), channel_id=2, replica_groups=mesh['dp'=8,'tensor'=4] {'tensor'}, dimensions={0}, use_global_device_ids=true | all-gather | bytes 23040 | tf_op jit(solution)/shard_map/all_gather | solution.py:125
  27.0 17.7 %all_gather.19 = bf16[512,768]{1,0:T(8,128)(2,1)S(1)} all-gather(bf16[128,768]{1,0:T(8,128)(2,1)S(1)} %fusion.33), channel_id=1, replica_groups=mesh['dp'=8,'tensor'=4] {'tensor'}, dimensions={0}, use_global_device_ids=true | all-gather | bytes 983040 | tf_op jit(solution)/shard_map/all_gather | solution.py:136
  44.7 0.7 fusion.104
  49.2 0.6 copy-done.40
  49.9 1.6 fusion.50
  51.5 35.6 %reduce-scatter.16.cloned.1.call-done = f32[128,768]{1,0:T(8,128)} async-done(((f32[512,768]{1,0:T(8,128)}), f32[128,768]{1,0:T(8,128)}) %reduce-scatter.16.cloned.1.call-update) | async-done | bytes 393232 | tf_op jit(solution)/shard_map/reduce_scatter | solution.py:150
  87.1 1.3 fusion.99
  88.5 2.2 fusion.40
  90.7 0.9 stack.38
  91.7 4.2 all-to-all-start
  95.9 33.7 %all_gather.20 = bf16[512,768]{1,0:T(8,128)(2,1)S(1)} all-gather(bf16[128,768]{1,0:T(8,128)(2,1)} %get-tuple-element.91), channel_id=1, replica_groups=mesh['dp'=8,'tensor'=4] {'tensor'}, dimensions={0}, use_global_device_ids=true | all-gather | bytes 983040 | tf_op jit(solution)/shard_map/all_gather | solution.py:184
  129.6 0.9 copy-done.11
  130.5 3.3 fusion.105
  133.8 5.5 %convert_reduce_fusion.1 = (f32[768]{0:T(1024)}, bf16[512,768]{1,0:T(8,128)(2,1)S(1)}, f32[512,768]{1,0:T(8,128)}) fusion(f32[512,768]{1,0:T(8,128)} %fusion.105, f32[768]{0:T(1024)S(1)} %copy-done.64, bf16[512,768]{1,0:T(8,128)(2,1)} %bitcast.10, bf16[768,768]{1,0:T(8,128)(2,1)} %param.21), kind=kOutput, calls=%fused_computation.11 | convolution fusion | flops 613022976 | bytes 5904384 | tf_op jit(solution)/shard_map/dot_general | solution.py:28
  139.3 0.9 copy-done.26
  140.2 2.0 fusion.106
  142.3 3.8 convolution_convert_fusion
  146.1 0.7 log_add_fusion.1
  146.8 0.7 log_add_fusion.2
  147.5 30.5 %reduce-scatter.20.cloned.1.call-done = f32[128,768]{1,0:T(8,128)} async-done(((f32[512,768]{1,0:T(8,128)}), f32[128,768]{1,0:T(8,128)}) %reduce-scatter.20.cloned.1.call-update) | async-done | bytes 393232 | tf_op jit(solution)/shard_map/reduce_scatter | solution.py:192
  178.1 1.3 fusion.95
  179.4 0.5 broadcast_multiply_fusion.3
  179.9 22.8 %reduce-scatter.18.cloned.1.call-done = bf16[128,768]{1,0:T(8,128)(2,1)} async-done(((bf16[512,768]{1,0:T(8,128)(2,1)}), bf16[128,768]{1,0:T(8,128)(2,1)}) %reduce-scatter.18.cloned.1.call-update) | async-done | bytes 196624 | tf_op jit(solution)/shard_map/reduce_scatter | solution.py:170
  202.7 2.5 multiply_convert_fusion.4
  205.2 18.3 %all_gather.21 = bf16[512,768]{1,0:T(8,128)(2,1)S(1)} all-gather(bf16[128,768]{1,0:T(8,128)(2,1)S(1)} %get-tuple-element.86), channel_id=1, replica_groups=mesh['dp'=8,'tensor'=4] {'tensor'}, dimensions={0}, use_global_device_ids=true | all-gather | bytes 983040 | tf_op jit(solution)/shard_map/all_gather | solution.py:202
  223.5 0.4 convolution_convert_fusion.1
  224.3 0.4 multiply_reduce_fusion
  224.9 0.6 copy-done.14
  226.4 0.4 multiply_reduce_fusion.1
  229.3 0.4 copy-done.42
  229.8 0.7 copy-done.43
  230.5 2.0 convolution_bitcast_fusion.2
  232.6 1.1 copy-done.7
  233.6 1.4 convolution_bitcast_fusion.3
  235.2 3.2 convolution_bitcast_fusion.1
  238.3 4.2 copy.29
  242.6 4.7 reshape.178
  247.3 19.9 %reduce-scatter.22.cloned.1.call-done = f32[128,768]{1,0:T(8,128)} async-done(((f32[512,768]{1,0:T(8,128)}), f32[128,768]{1,0:T(8,128)}) %reduce-scatter.22.cloned.1.call-update) | async-done | bytes 393232 | tf_op jit(solution)/shard_map/reduce_scatter | solution.py:220
  267.2 1.4 fusion.96
  268.7 2.0 fusion.38
  271.0 0.7 copy-done.17
  271.8 3.5 convolution_bitcast_fusion
  275.3 4.2 fusion.97
  279.6 3.6 fusion.107
  283.3 0.6 copy-done.50
  283.9 9.2 %all-gather.2 = f32[8,1,768]{2,1,0:T(1,128)S(1)} all-gather(f32[1,1,768]{2,1,0:T(1,128)S(1)} %bitcast_convert_fusion), channel_id=1, replica_groups=mesh['dp'=8,'tensor'=4] {'dp'}, dimensions={0}, use_global_device_ids=true | all-gather | bytes 27648 | tf_op jit(solution)/shard_map/all_gather | solution.py:250
  293.2 1.3 convert_reduce_fusion
  295.0 9.2 %reduce-scatter.32.cloned.1.call-done = f32[96,192]{1,0:T(8,128)} async-done(((f32[768,192]{1,0:T(8,128)}), f32[96,192]{1,0:T(8,128)}) %reduce-scatter.32.cloned.1.call-update) | async-done | bytes 73744
  304.2 1.6 copy.32
  305.8 41.9 %reduce-scatter.30.cloned.1.call-done = f32[96,576]{1,0:T(8,128)} async-done(((f32[768,576]{1,0:T(8,128)}), f32[96,576]{1,0:T(8,128)}) %reduce-scatter.30.cloned.1.call-update) | async-done | bytes 221200
  347.8 1.1 reshape.179
  348.9 0.8 copy.26
  349.7 48.6 %reduce-scatter.28.cloned.1.call-done = f32[1152,1]{1,0:T(8,128)} async-done(((f32[4608,1]{1,0:T(8,128)}), f32[1152,1]{1,0:T(8,128)}) %reduce-scatter.28.cloned.1.call-update) | async-done | bytes 4624
  398.2 1.3 copy.28
  399.5 1.3 bitcast_reduce_fusion
  400.9 24.4 %all-reduce = (f32[1152]{0:T(1024)}, f32[2,192]{1,0:T(2,128)}, f32[768]{0:T(1024)}, f32[768]{0:T(1024)}, f32[768]{0:T(1024)}) all-reduce(f32[1152]{0:T(1024)S(1)} %bitcast_reduce_fusion, f32[2,192]{1,0:T(2,128)S(1)} %pad_maximum_fusion.6, f32[768]{0:T(1024)S(1)} %convert_reduce_fusion.2, ...), channel_id=1, replica_groups=mesh['dp'=8,'tensor'=4] {'dp'}, use_global_device_ids=true, to_apply=%region_22.23 | all-reduce | flops 3840 | bytes 30720 | tf_op jit(solution)/shard_map/psum | solution.py:245
  425.3 8.1 %all-gather.3 = f32[8,1,1152]{2,1,0:T(1,128)S(1)} all-gather(f32[1,1,1152]{2,1,0:T(1,128)S(1)} %bitcast.99), channel_id=1, replica_groups=mesh['dp'=8,'tensor'=4] {'dp'}, dimensions={0}, use_global_device_ids=true | all-gather | bytes 41472 | tf_op jit(solution)/shard_map/all_gather | solution.py:251
  433.4 1.3 fusion.78
  434.7 10.0 %reduce-scatter.26.cloned.1.call-done = f32[768,96]{0,1:T(8,128)} async-done(((f32[768,768]{0,1:T(8,128)}), f32[768,96]{0,1:T(8,128)}) %reduce-scatter.26.cloned.1.call-update) | async-done | bytes 294928 | tf_op jit(solution)/shard_map/reduce_scatter | solution.py:260
  444.7 46.5 %reduce-scatter.24.cloned.1.call-done = f32[96,768]{1,0:T(8,128)} async-done(((f32[768,768]{1,0:T(8,128)}), f32[96,768]{1,0:T(8,128)}) %reduce-scatter.24.cloned.1.call-update) | async-done | bytes 294928 | tf_op jit(solution)/shard_map/reduce_scatter | solution.py:259
  (192 shorter events, 9.8 us)
Async XLA Ops:
  7.2 3.2 copy-start
  7.2 4.2 copy-start.57
  7.2 79.8 %reduce-scatter.16.cloned.1.call-start = ((), (), s32[]{:S(2)}) async-start(), calls=%async_computation.10 | async-start | bytes 1966080 | tf_op jit(solution)/shard_map/reduce_scatter | solution.py:150
  8.4 18.3 %copy-start.51 = (f32[128]{0:T(128)}, f32[128]{0:T(128)S(1)}, u32[]{:S(2)}) copy-start(f32[128]{0:T(128)S(1)} %broadcast_multiply_fusion.6) | copy-start | bytes 1540
  9.6 17.2 %copy-start.60 = (f32[128]{0:T(128)}, f32[128]{0:T(128)S(1)}, u32[]{:S(2)}) copy-start(f32[128]{0:T(128)S(1)} %add_rsqrt_fusion.1) | copy-start | bytes 1540
  11.4 15.4 %copy-start.8 = (bf16[128,768]{1,0:T(8,128)(2,1)S(1)}, bf16[128,768]{1,0:T(8,128)(2,1)}, u32[]{:S(2)}) copy-start(bf16[128,768]{1,0:T(8,128)(2,1)} %param.13) | copy-start | bytes 589828
  26.8 18.6 %copy-start.5 = (f32[128,4608]{1,0:T(8,128)}, f32[128,4608]{1,0:T(8,128)S(1)}, u32[]{:S(2)}) copy-start(f32[128,4608]{1,0:T(8,128)S(1)} %broadcast_multiply_fusion) | copy-start | bytes 7077892
  26.8 18.0 %copy-start.22 = (bf16[3,768,192]{1,2,0:T(8,128)(2,1)S(1)}, bf16[3,768,192]{1,2,0:T(8,128)(2,1)}, u32[]{:S(2)}) copy-start(bf16[3,768,192]{1,2,0:T(8,128)(2,1)} %param.17) | copy-start | bytes 2654212
  45.7 1.1 copy-start.15
  45.8 2.9 copy-start.24
  46.1 1.0 copy-start.3
  46.5 1.4 copy-start.1
  46.9 1.8 copy-start.44
  48.7 1.2 copy-start.20
  49.8 37.2 %copy-start.45 = (f32[768]{0:T(1024)S(1)}, f32[768]{0:T(1024)}, u32[]{:S(2)}) copy-start(f32[768]{0:T(1024)} %param.20) | copy-start | bytes 9220
  88.3 3.3 copy-start.48
  88.5 3.1 copy-start.58
  91.7 42.1 %all-to-all-start = ((bf16[4,128,768]{2,1,0:T(8,128)(2,1)}), bf16[4,128,768]{2,1,0:T(8,128)(2,1)}, u32[]{:S(2)}, u32[]{:S(2)}) async-start(bf16[4,128,768]{2,1,0:T(8,128)(2,1)} %stack.38), calls=%async_computation.1 | async-start | bytes 1572864 | tf_op jit(solution)/shard_map/all_to_all | solution.py:165
  95.9 82.2 %reduce-scatter.20.cloned.1.call-start = ((), (), s32[]{:S(2)}) async-start(), calls=%async_computation.12 | async-start | bytes 1966080 | tf_op jit(solution)/shard_map/reduce_scatter | solution.py:192
  129.6 0.9 copy-start.11
  130.5 3.3 copy-start.64
  133.8 6.4 %copy-start.63 = (bf16[768,768]{1,0:T(8,128)(2,1)S(1)}, bf16[768,768]{1,0:T(8,128)(2,1)}, u32[]{:S(2)}) copy-start(bf16[768,768]{1,0:T(8,128)(2,1)} %param.21) | copy-start | bytes 3538948
  142.2 60.5 %reduce-scatter.18.cloned.1.call-start = ((), (), s32[]{:S(2)}) async-start(), calls=%async_computation.11 | async-start | bytes 983040 | tf_op jit(solution)/shard_map/reduce_scatter | solution.py:170
  142.2 3.9 copy-start.54
  146.1 121.2 %reduce-scatter.22.cloned.1.call-start = ((), (), s32[]{:S(2)}) async-start(), calls=%async_computation.13 | async-start | bytes 1966080 | tf_op jit(solution)/shard_map/reduce_scatter | solution.py:220
  202.7 20.8 %copy-start.21 = (bf16[192,768]{1,0:T(8,128)(2,1)S(1)}, bf16[192,768]{1,0:T(8,128)(2,1)}, u32[]{:S(2)}) copy-start(bf16[192,768]{1,0:T(8,128)(2,1)} %param.19) | copy-start | bytes 884740
  205.2 18.7 %copy-start.4 = (f32[512,512]{0,1:T(8,128)S(1)}, f32[512,512]{0,1:T(8,128)}, u32[]{:S(2)}) copy-start(f32[512,512]{0,1:T(8,128)} %copy-done.3) | copy-start | bytes 3145732
  205.2 19.0 %copy-start.25 = (bf16[512,192]{0,1:T(8,128)(2,1)S(1)}, bf16[512,192]{0,1:T(8,128)(2,1)}, u32[]{:S(2)}) copy-start(bf16[512,192]{0,1:T(8,128)(2,1)} %copy-done.24) | copy-start | bytes 589828
  223.5 1.1 copy-start.6
  224.3 4.8 copy-start.28
  224.6 0.9 copy-start.14
  224.7 1.1 copy-start.16
  224.7 1.4 copy-start.2
  225.8 3.3 copy-start.30
  226.4 2.6 copy-start.32
  227.3 1.8 copy-start.34
  227.8 1.2 copy-start.36
  228.5 2.0 copy-start.23
  232.5 1.1 copy-start.7
  232.5 1.1 copy-start.41
  232.5 71.7 %reduce-scatter.32.cloned.1.call-start = ((), (), s32[]{:S(2)}) async-start(), calls=%async_computation.18 | async-start | bytes 884736
  235.1 112.7 %reduce-scatter.30.cloned.1.call-start = ((), (), s32[]{:S(2)}) async-start(), calls=%async_computation.17 | async-start | bytes 2211840
  247.2 20.0 %copy-start.52 = (f32[128]{0:T(128)S(1)}, f32[128]{0:T(128)}, u32[]{:S(2)}) copy-start(f32[128]{0:T(128)} %copy-done.51) | copy-start | bytes 1540
  247.2 20.0 %copy-start.61 = (f32[128]{0:T(128)S(1)}, f32[128]{0:T(128)}, u32[]{:S(2)}) copy-start(f32[128]{0:T(128)} %copy-done.60) | copy-start | bytes 1540
  247.2 21.4 %copy-start.10 = (f32[128,768]{1,0:T(8,128)S(1)}, f32[128,768]{1,0:T(8,128)}, u32[]{:S(2)}) copy-start(f32[128,768]{1,0:T(8,128)} %get-tuple-element.87) | copy-start | bytes 1179652
  247.3 23.4 %copy-start.46 = (f32[768]{0:T(1024)S(1)}, f32[768]{0:T(1024)}, u32[]{:S(2)}) copy-start(f32[768]{0:T(1024)} %param.20) | copy-start | bytes 9220
  247.3 151.0 %reduce-scatter.28.cloned.1.call-start = ((), (), s32[]{:S(2)}) async-start(), calls=%async_computation.16 | async-start | bytes 2949120
  267.2 1.4 copy-start.18
  267.2 3.5 copy-start.19
  268.7 2.1 copy-start.9
  268.7 2.2 copy-start.49
  268.7 2.2 copy-start.59
  270.7 0.9 copy-start.17
  270.7 1.0 copy-start.27
  270.7 1.0 copy-start.47
  275.3 169.4 %reduce-scatter.26.cloned.1.call-start = ((), (), s32[]{:S(2)}) async-start(), calls=%async_computation.15 | async-start | bytes 2654208 | tf_op jit(solution)/shard_map/reduce_scatter | solution.py:260
  279.6 211.6 %reduce-scatter.24.cloned.1.call-start = ((), (), s32[]{:S(2)}) async-start(), calls=%async_computation.14 | async-start | bytes 2654208 | tf_op jit(solution)/shard_map/reduce_scatter | solution.py:259
  283.2 11.3 %copy-start.29 = (bf16[512,64]{0,1:T(8,128)(2,1)S(1)}, bf16[512,64]{0,1:T(8,128)(2,1)}, u32[]{:S(2)}) copy-start(bf16[512,64]{0,1:T(8,128)(2,1)} %copy-done.28) | copy-start | bytes 196612
  283.2 11.3 %copy-start.33 = (bf16[512,64]{0,1:T(8,128)(2,1)S(1)}, bf16[512,64]{0,1:T(8,128)(2,1)}, u32[]{:S(2)}) copy-start(bf16[512,64]{0,1:T(8,128)(2,1)} %copy-done.32) | copy-start | bytes 196612
  283.2 11.3 %copy-start.37 = (bf16[512,64]{0,1:T(8,128)(2,1)S(1)}, bf16[512,64]{0,1:T(8,128)(2,1)}, u32[]{:S(2)}) copy-start(bf16[512,64]{0,1:T(8,128)(2,1)} %copy-done.36) | copy-start | bytes 196612
  283.2 11.4 %copy-start.31 = (bf16[512,64]{0,1:T(8,128)(2,1)S(1)}, bf16[512,64]{0,1:T(8,128)(2,1)}, u32[]{:S(2)}) copy-start(bf16[512,64]{0,1:T(8,128)(2,1)} %copy-done.30) | copy-start | bytes 196612
  283.2 11.4 %copy-start.35 = (bf16[512,64]{0,1:T(8,128)(2,1)S(1)}, bf16[512,64]{0,1:T(8,128)(2,1)}, u32[]{:S(2)}) copy-start(bf16[512,64]{0,1:T(8,128)(2,1)} %copy-done.34) | copy-start | bytes 196612
  283.3 11.4 %copy-start.39 = (bf16[512,64]{0,1:T(8,128)(2,1)S(1)}, bf16[512,64]{0,1:T(8,128)(2,1)}, u32[]{:S(2)}) copy-start(bf16[512,64]{0,1:T(8,128)(2,1)} %copy-done.38) | copy-start | bytes 196612
  294.8 106.0 %copy-start.62 = (f32[768]{0:T(1024)S(1)}, f32[768]{0:T(1024)}, u32[]{:S(2)}) copy-start(f32[768]{0:T(1024)} %get-tuple-element.84) | copy-start | bytes 9220
  (11 other events, 7.7 us)
Sparse Core Ops, SparseCore 0:
  51.6 35.4 reduce-scatter.15
  142.3 35.6 reduce-scatter.19
  180.4 22.2 reduce-scatter.17
  232.7 34.5 reduce-scatter.21
  270.2 33.9 reduce-scatter.31
  307.5 40.2 reduce-scatter.29
  350.2 48.0 reduce-scatter.27
  402.5 42.1 reduce-scatter.25
  448.6 42.4 reduce-scatter.23
